TPU v7x, 256 devices: a whole 4x4x8 slice. The times are simulated.
256 devices in a mesh: dp: 64 (over z, x, core), proto: 4 (over y).
Axes of the slice: x: 4, y: 4, z: 8, core: 2. Of those that a mesh axis runs over, the one named last changes fastest.
Arguments:
- student_feat: bfloat16 [16384, 256], P('dp')
- teacher_feat: bfloat16 [16384, 256], P('dp')
- proto_weight: float32 [65536, 256], P(('proto', 'dp'))
Outputs:
- grad_student: float32 [16384, 256], P('dp')
- grad_proto: float32 [65536, 256], P(('proto', 'dp'))
- loss: float32 [], replicated
All inputs are finite; a program needn't handle non-finite values.
Results may differ from a plain program's by a relative error of at most 0.0024.
Values may be sent and summed in bfloat16 or wider, within the bound.
A program may use at most 128 MiB of HBM per device.

v0:
```python
import jax
import jax.numpy as jnp
from jax import lax
from jax.sharding import PartitionSpec as P

SWEEPS = 3


teacher_temp = 0.04
student_temp = 0.1
loss_scale = 1024.0
epsilon = 1e-06
precise = lax.Precision.HIGHEST
contract_last = (((1,), (1,)), ((), ()))
contract_first = (((0,), (0,)), ((), ()))


def unit_rows(values):
    wide_values = values.astype(jnp.float32)
    return wide_values * lax.rsqrt(
        jnp.sum(wide_values * wide_values, axis=1, keepdims=True) + epsilon
    )


def unit_back(values, upstream):
    wide_values = values.astype(jnp.float32)
    inverse = lax.rsqrt(jnp.sum(wide_values * wide_values, axis=1, keepdims=True) + epsilon)
    direction = wide_values * inverse
    return (upstream - direction * jnp.sum(direction * upstream, axis=1, keepdims=True)) * inverse


def by_weights(student_unit, teacher_unit, proto_unit):
    protos = lax.all_gather(proto_unit, "dp", axis=0, tiled=True)
    teach_exp = jnp.exp(
        lax.dot_general(teacher_unit, protos, contract_last, preferred_element_type=jnp.float32)
        / teacher_temp
    )
    student_logits = (
        lax.dot_general(student_unit, protos, contract_last, preferred_element_type=jnp.float32)
        / student_temp
    )
    stud_sum = jnp.sum(jnp.exp(student_logits), axis=1)
    log_total = jnp.log(lax.psum(stud_sum, "proto"))
    crop_weight = jnp.ones((teach_exp.shape[0],), jnp.float32)
    for sweep_index in range(SWEEPS):
        column_sum = lax.psum(jnp.dot(crop_weight, teach_exp, precision=precise), "dp")
        column_scale = 1.0 / column_sum
        row_part = jnp.dot(teach_exp, column_scale, precision=precise)
        crop_weight = 1.0 / lax.psum(row_part, "proto")
    assign = crop_weight[:, None] * teach_exp * column_scale[None, :]
    shifted = student_logits - log_total[:, None]
    loss_part = jnp.sum(assign * shifted)
    gradient = (loss_scale * (jnp.exp(shifted) - assign)).astype(jnp.bfloat16)
    grad_unit = lax.psum(jnp.dot(gradient, protos, preferred_element_type=jnp.float32), "proto")
    proto_rows = lax.psum_scatter(
        lax.dot_general(gradient, student_unit, contract_first, preferred_element_type=jnp.float32),
        "dp",
        scatter_dimension=0,
        tiled=True,
    )
    loss_sum = lax.psum(loss_part, ("dp", "proto"))
    return (grad_unit, proto_rows, loss_sum)


def shards(student_feat, teacher_feat, proto_weight):
    student_unit = unit_rows(student_feat).astype(jnp.bfloat16)
    teacher_unit = unit_rows(teacher_feat).astype(jnp.bfloat16)
    proto_unit = unit_rows(proto_weight).astype(jnp.bfloat16)
    crop_count = lax.axis_size("dp") * student_unit.shape[0]
    grad_unit, proto_rows, loss_sum = by_weights(student_unit, teacher_unit, proto_unit)
    grad_student = unit_back(student_feat, grad_unit)
    grad_proto = unit_back(proto_weight, proto_rows)
    loss = -loss_sum / crop_count
    return (grad_student, grad_proto, loss)


def solution(mesh):
    return jax.shard_map(
        shards,
        mesh=mesh,
        in_specs=(P("dp", None), P("dp", None), P(("proto", "dp"), None)),
        out_specs=(P("dp", None), P(("proto", "dp"), None), P()),
        check_vma=False,
    )
```

profile of v0, /device:TPU:1, one launch (start us, length us, event | category | flops | bytes accessed | tf_op | source)
XLA Modules:
  0.0 987.1 jit_solution(12838253682589509145)
XLA Ops:
  8.3 1.7 multiply_convert_fusion.1
  11.1 87.5 %all-gather.2.cloned.1.call-done = bf16[16384,256]{1,0:T(8,128)(2,1)} async-done(((bf16[256,256]{1,0:T(8,128)(2,1)}), bf16[16384,256]{1,0:T(8,128)(2,1)}) %all-gather.2.cloned.1.call-update) | async-done | bytes 8388624 | tf_op jit(solution)/shard_map/all_gather | solution.py:33
  98.6 11.8 %fusion = f32[256,16384]{1,0:T(8,128)} fusion(bf16[16384,256]{1,0:T(8,128)(2,1)} %all-gather.2.cloned.1.call-done, bf16[256,256]{1,0:T(8,128)(2,1)} %param.4, f32[256]{0:T(256)S(1)} %add_rsqrt_fusion), kind=kOutput, calls=%fused_computation.1 | convolution fusion | flops 2151874560 | bytes 25297920 | tf_op jit(solution)/shard_map/dot_general | solution.py:35
  110.4 12.1 %fusion.15 = f32[1,16384]{1,0:T(1,128)} fusion(f32[256,16384]{1,0:T(8,128)} %fusion), kind=kOutput, calls=%fused_computation.32 | convolution fusion | flops 50331648 | bytes 16842752 | tf_op jit(solution)/shard_map/dot_general | solution.py:46
  122.6 164.8 %all-reduce.6.cloned.1.call-done = f32[16384]{0:T(1024)} async-done(((f32[16384]{0:T(1024)}), f32[16384]{0:T(1024)}) %all-reduce.6.cloned.1.call-update) | async-done | bytes 65552 | tf_op jit(solution)/shard_map/psum | solution.py:46
  288.3 16.1 %fusion.18 = f32[1,256]{1,0:T(1,128)S(1)} fusion(f32[256,16384]{1,0:T(8,128)} %fusion, f32[16384,1]{0,1:T(1,128)S(1)} %bitcast.31), kind=kOutput, calls=%fused_computation.38 | convolution fusion | flops 50331648 | bytes 16843776 | tf_op jit(solution)/shard_map/dot_general | solution.py:48
  304.4 8.9 psum.65
  313.3 12.1 %fusion.19 = f32[1,16384]{1,0:T(1,128)} fusion(f32[256,1]{0,1:T(1,128)S(1)} %bitcast.35, f32[256,16384]{1,0:T(8,128)} %fusion), kind=kOutput, calls=%fused_computation.39 | convolution fusion | flops 50331648 | bytes 16843776 | tf_op jit(solution)/shard_map/dot_general | solution.py:46
  325.4 165.1 %all-reduce.8.cloned.1.call-done = f32[16384]{0:T(1024)} async-done(((f32[16384]{0:T(1024)}), f32[16384]{0:T(1024)}) %all-reduce.8.cloned.1.call-update) | async-done | bytes 65552 | tf_op jit(solution)/shard_map/psum | solution.py:46
  491.4 16.1 %fusion.20 = f32[1,256]{1,0:T(1,128)S(1)} fusion(f32[256,16384]{1,0:T(8,128)} %fusion, f32[16384,1]{0,1:T(1,128)S(1)} %bitcast.32), kind=kOutput, calls=%fused_computation.40 | convolution fusion | flops 50331648 | bytes 16843776 | tf_op jit(solution)/shard_map/dot_general | solution.py:48
  507.4 8.6 psum.67
  516.1 12.1 %fusion.21 = f32[1,16384]{1,0:T(1,128)} fusion(f32[256,1]{0,1:T(1,128)S(1)} %bitcast.37, f32[256,16384]{1,0:T(8,128)} %fusion), kind=kOutput, calls=%fused_computation.41 | convolution fusion | flops 50331648 | bytes 16843776 | tf_op jit(solution)/shard_map/dot_general | solution.py:46
  528.2 12.4 %exponential_reduce_fusion = (f32[256]{0:T(256)S(1)}, f32[256,16384]{1,0:T(8,128)}) fusion(bf16[16384,256]{1,0:T(8,128)(2,1)} %all-gather.2.cloned.1.call-done, bf16[256,256]{1,0:T(8,128)(2,1)S(1)} %copy-done.2, f32[256]{0:T(256)S(1)} %add_rsqrt_fusion.2), kind=kOutput, calls=%fused_computation.6 | convolution fusion | flops 2156068608 | bytes 25298944 | tf_op jit(solution)/shard_map/dot_general | solution.py:39
  540.6 152.7 %all-reduce.10.cloned.1.call-done = f32[16384]{0:T(1024)} async-done(((f32[16384]{0:T(1024)}), f32[16384]{0:T(1024)}) %all-reduce.10.cloned.1.call-update) | async-done | bytes 65552 | tf_op jit(solution)/shard_map/psum | solution.py:46
  694.2 16.1 %fusion.22 = f32[1,256]{1,0:T(1,128)S(1)} fusion(f32[256,16384]{1,0:T(8,128)} %fusion, f32[16384,1]{0,1:T(1,128)S(1)} %bitcast.27), kind=kOutput, calls=%fused_computation.42 | convolution fusion | flops 50331648 | bytes 16843776 | tf_op jit(solution)/shard_map/dot_general | solution.py:48
  710.2 8.7 all-reduce
  718.9 12.8 %multiply_reduce_fusion = (f32[]{:T(128)}, bf16[256,16384]{1,0:T(8,128)(2,1)S(1)}) fusion(f32[256,16384]{1,0:T(8,128)} %get-tuple-element.8, f32[256,16384]{1,0:T(8,128)} %fusion, f32[16384]{0:T(1024)S(1)} %broadcast_divide_fusion, f32[256]{0:T(256)S(1)} %broadcast_divide_fusion.5, f32[256]{0:T(256)S(1)} %log.3), kind=kLoop, calls=%fused_computation.3 | loop fusion | flops 33554432 | bytes 42010628 | tf_op jit(solution)/shard_map/reduce_sum | solution.py:52
  731.7 3.2 copy-done
  735.0 6.5 fusion.23
  741.5 11.6 %fusion.12 = f32[16384,256]{1,0:T(8,128)} fusion(bf16[256,16384]{1,0:T(8,128)(2,1)} %copy-done, bf16[256,256]{1,0:T(8,128)(2,1)S(1)} %copy-done.2, f32[256]{0:T(256)S(1)} %add_rsqrt_fusion.2), kind=kOutput, calls=%fused_computation.25 | convolution fusion | flops 2147680256 | bytes 25297920 | tf_op jit(solution)/shard_map/dot_general | solution.py:56
  753.1 75.3 %psum.71 = f32[]{:T(128)} all-reduce(f32[]{:T(128)} %get-tuple-element.5), channel_id=1, replica_groups=mesh['dp'=64,'proto'=4] {'dp','proto'}, use_global_device_ids=true, to_apply=%region_16.0 | all-reduce | flops 1 | bytes 8 | tf_op jit(solution)/shard_map/psum | solution.py:61
  830.3 1.8 fusion.6
  832.1 143.9 %reduce-scatter.2.cloned.1.call-done = f32[256,256]{1,0:T(8,128)} async-done(((f32[16384,256]{1,0:T(8,128)}), f32[256,256]{1,0:T(8,128)}) %reduce-scatter.2.cloned.1.call-update) | async-done | bytes 262160 | tf_op jit(solution)/shard_map/reduce_scatter | solution.py:55
  977.1 1.8 subtract_multiply_fusion
  (33 shorter events, 7.4 us)
Async XLA Ops:
  7.2 91.4 %all-gather.2.cloned.1.call-start = ((), (), s32[]{:S(2)}) async-start(), calls=%async_computation.1 | async-start | bytes 8519680 | tf_op jit(solution)/shard_map/all_gather | solution.py:33
  10.0 277.4 %all-reduce.6.cloned.1.call-start = ((), (), s32[]{:S(2)}) async-start(), calls=%async_computation.2 | async-start | bytes 131072 | tf_op jit(solution)/shard_map/psum | solution.py:46
  11.1 111.4 %copy-start.2 = (bf16[256,256]{1,0:T(8,128)(2,1)S(1)}, bf16[256,256]{1,0:T(8,128)(2,1)}, u32[]{:S(2)}) copy-start(bf16[256,256]{1,0:T(8,128)(2,1)} %param.3) | copy-start | bytes 393220
  122.4 368.1 %all-reduce.8.cloned.1.call-start = ((), (), s32[]{:S(2)}) async-start(), calls=%async_computation.3 | async-start | bytes 131072 | tf_op jit(solution)/shard_map/psum | solution.py:46
  325.4 367.9 %all-reduce.10.cloned.1.call-start = ((), (), s32[]{:S(2)}) async-start(), calls=%async_computation.4 | async-start | bytes 131072 | tf_op jit(solution)/shard_map/psum | solution.py:46
  528.2 301.0 %all-reduce.12.cloned.1.call-start = ((), (), s32[]{:S(2)}) async-start(), calls=%async_computation.5 | async-start | bytes 524288 | tf_op jit(solution)/shard_map/psum | solution.py:54
  731.7 3.2 copy-start
  741.5 234.5 %reduce-scatter.2.cloned.1.call-start = ((), (), s32[]{:S(2)}) async-start(), calls=%async_computation.6 | async-start | bytes 17039360 | tf_op jit(solution)/shard_map/reduce_scatter | solution.py:55
  753.1 222.9 %copy-start.1 = (f32[256,256]{1,0:T(8,128)S(1)}, f32[256,256]{1,0:T(8,128)}, u32[]{:S(2)}) copy-start(f32[256,256]{1,0:T(8,128)} %param.5) | copy-start | bytes 786436
Sparse Core Ops, SparseCore 0:
  11.3 87.1 all-gather.1
  122.6 164.8 all-reduce.5
  325.5 164.9 all-reduce.7
  528.3 164.9 all-reduce.9
  741.6 41.4 all-reduce.11
  788.1 187.8 reduce-scatter.1
where the time goes:
time: 999 us; the launch traced here: 987 us
  waiting for transfers between devices  714 us (71%)
  matrix products  127 us (13%)
  blocking collectives  102 us (10%)
  other arithmetic  25.2 us (3%)
  between operations  16.2 us (2%)
    psum x3, waiting for transfers between devices, by_weights(): lax.psum(jnp.dot(crop_weight, teach_exp, precision=precise), 'dp')  483 us
    reduce_scatter x1, waiting for transfers between devices, by_weights(): lax.psum_scatter(lax.dot_general(gradient, student_unit, contract_first,...  144 us
    all_gather x1, waiting for transfers between devices, by_weights(): protos = lax.all_gather(proto_unit, 'dp', axis=0, tiled=True)  87.5 us
    psum x1, blocking collectives, by_weights(): loss_sum = lax.psum(loss_part, ('dp', 'proto'))  75.3 us
    dot_general x3, matrix products, by_weights(): row_part = jnp.dot(teach_exp, column_scale, precision=precise)  48.2 us
    dot_general x3, matrix products, by_weights(): jnp.dot(crop_weight, teach_exp, precision=precise)  36.2 us
    psum x3, blocking collectives, by_weights(): crop_weight = 1.0 / lax.psum(row_part, 'proto')  26.2 us
  transfers between devices with their start and end apart: 6, of which 5 were waited for; matrix products, arithmetic and copies ran while one was open for 3% of the time, Pallas kernels for 0%

commit v1 on v0

v1 whole, which is shorter than its diff:
```python
import functools
import itertools

import jax
import jax.numpy as jnp
from jax import lax
from jax.experimental import pallas as pl
from jax.experimental.pallas import tpu as pltpu
from jax.sharding import PartitionSpec as P

SWEEPS = 3
X, Y, C = 4, 4, 2
B = 256
D = 256
L = 128
NB = X * C
CR = NB * B
Q = B // Y
LOG2E = 1.4426950408889634
EPS = 1e-6
F32, BF16 = jnp.float32, jnp.bfloat16
MESH = pl.DeviceIdType.MESH
NT = (((1,), (1,)), ((), ()))


def inverse_norm(v):
    return lax.rsqrt(jnp.sum(v * v, axis=1, keepdims=True) + EPS)


def unit_back(v, upstream):
    inv = inverse_norm(v)
    u = v * inv
    return (upstream - u * jnp.sum(u * upstream, axis=1, keepdims=True)) * inv


def ring_distance(d, n):
    return min(d, n - d)


def offsets(sizes):
    every = [o for o in itertools.product(*[range(n) for n in sizes]) if any(o)]
    return sorted(every, key=lambda o: -sum(ring_distance(d, n) for d, n in zip(o, sizes)))


def kernel(Z, sf, tf, pw, gs_o, gp_o, loss_o, T, U, PR, K, S, G, UT, cwb, ltb, part, col, colr, row0, row0r, row, rowr,
           pg, pgr, gu, corer, rsr, gsb, lz, lzr, lx, lxr, cscale, ssem, rsem, csem, xsem):
    H = Z // 2
    dp, y = lax.axis_index("dp"), lax.axis_index("proto")
    z, x, c = dp // (X * C), lax.rem(dp // C, X), lax.rem(dp, C)

    def dev(zz, xx, yy, cc):
        return ((zz * X + xx) * C + cc, yy)

    def at_z(d):
        return dev(lax.rem(z + d, Z), x, y, c)

    def at_xyc(o):
        return dev(z, lax.rem(x + o[0], X), lax.rem(y + o[1], Y), lax.rem(c + o[2], C))

    z_offs = [o[0] for o in offsets((Z,))]
    xyc_offs = offsets((X, Y, C))
    xy_offs = offsets((X, Y))
    partner = at_xyc((0, 0, 1))

    barrier = pltpu.get_barrier_semaphore()
    for d in z_offs:
        pl.semaphore_signal(barrier, 1, device_id=at_z(d), device_id_type=MESH)
    for o in xyc_offs:
        pl.semaphore_signal(barrier, 1, device_id=at_xyc(o), device_id_type=MESH)

    own = x * C + c
    pv = pw[...]
    PR[z] = (pv * inverse_norm(pv)).astype(BF16)
    tv = tf[...].astype(F32)
    T[own] = (tv * inverse_norm(tv)).astype(BF16)
    sv = sf[...].astype(F32)
    U[own] = (sv * inverse_norm(sv)).astype(BF16)
    pl.semaphore_wait(barrier, len(z_offs) + len(xyc_offs))

    count = [0]
    sent = []

    def send(src, dst, device):
        i = count[0]
        count[0] += 1
        copy = pltpu.make_async_remote_copy(src, dst, ssem.at[i], rsem.at[i], device_id=device, device_id_type=MESH)
        copy.start()
        sent.append(copy)
        return copy

    def wait_bytes(ref, sem):
        pltpu.make_async_copy(ref, ref, sem).wait()

    def exchange(src, slots, targets, k):
        for i, device in enumerate(targets):
            pltpu.make_async_remote_copy(
                src, slots.at[i], xsem.at[k], csem.at[k], device_id=device, device_id_type=MESH
            ).start()

    def arrive(slots, k):
        wait_bytes(slots, csem.at[k])

    z_targets = [at_z(d) for d in z_offs]
    xyc_targets = [at_xyc(o) for o in xyc_offs]

    up, down = at_z(1), at_z(Z - 1)
    half = B // 2
    lo, hi = pl.ds(0, half), pl.ds(half, half)
    ring = []
    ring.append([(send(PR.at[z, part_rows], PR.at[z, part_rows], up), send(PR.at[z, part_rows], PR.at[z, part_rows], down))
                 for part_rows in (lo, hi)])

    x_offs = sorted(range(1, X), key=lambda d: -ring_distance(d, X))

    def spread(A):
        return [send(A.at[own], A.at[own], at_xyc((d, 0, 0))) for d in x_offs], [send(A.at[own], A.at[own], partner)]

    def pass_on(A, copies):
        got, to_partner = copies
        for d, copy in zip(x_offs, got):
            copy.wait_recv()
            b = lax.rem(x + X - d, X) * C + c
            to_partner.append(send(A.at[b], A.at[b], partner))

    t_copies = spread(T)
    u_copies = spread(U)
    pass_on(T, t_copies)

    def ring_step(s):
        up_z, down_z = lax.rem(z + Z - s, Z), lax.rem(z + s, Z)
        step = []
        for i, part_rows in enumerate((lo, hi)):
            pair = [None, None]
            if s < H:
                ring[s - 1][i][0].wait_recv()
                ring[s - 1][i][1].wait_recv()
                if s + 1 < H or i == 0:
                    pair[0] = send(PR.at[up_z, part_rows], PR.at[up_z, part_rows], up)
                if s + 1 < H or i == 1:
                    pair[1] = send(PR.at[down_z, part_rows], PR.at[down_z, part_rows], down)
            else:
                ring[s - 1][i][i].wait_recv()
            step.append(pair)
        ring.append(step)

    def teacher_block(zz):
        protos = PR[zz]

        def tile(b, acc):
            logits = lax.dot_general(T[b], protos, NT, preferred_element_type=F32)
            e = jnp.exp2(logits * (25.0 * LOG2E))
            K[zz, pl.ds(pl.multiple_of(b * B, B), B)] = e
            return acc + jnp.sum(e.reshape(B // 8, 8, B), axis=0)

        acc = lax.fori_loop(0, NB, tile, jnp.zeros((8, B), F32))
        col[0, pl.ds(zz, 1)] = jnp.sum(acc, axis=0, keepdims=True)

    for copy in t_copies[1]:
        copy.wait_recv()
    teacher_block(z)
    for s in range(1, H):
        ring_step(s)
        teacher_block(lax.rem(z + Z - s, Z))
        teacher_block(lax.rem(z + s, Z))
        if s == 1:
            pass_on(U, u_copies)
    ring_step(H)
    teacher_block(lax.rem(z + H, Z))
    exchange(col.at[0], colr.at[0], z_targets, 0)

    for copy in u_copies[1]:
        copy.wait_recv()

    def student_tile(b, carry):
        units = U[b]
        rows = pl.ds(pl.multiple_of(b * B, B), B)
        total = jnp.zeros((B, L), F32)
        for zz in range(Z):
            logits = lax.dot_general(units, PR[zz], NT, preferred_element_type=F32)
            S[zz, rows] = logits
            e = jnp.exp2(logits * (10.0 * LOG2E))
            total = total + e[:, :L] + e[:, L:]
        part[rows] = total
        UT[b] = units.T
        return carry

    lax.fori_loop(0, NB, student_tile, 0)
    ones = jnp.ones((8, L), F32)

    def to_lanes(dst, first):
        for b in range(NB):
            sums = lax.dot_general(ones, part[b * B:(b + 1) * B], NT, precision=lax.Precision.HIGHEST, preferred_element_type=F32)
            dst[first + b:first + b + 1, :] = sums[:1]

    def to_rows(dst, values):
        for b in range(NB):
            dst[b * B:(b + 1) * B, :] = jnp.broadcast_to(values[b:b + 1], (L, B)).T

    to_lanes(row0, NB)

    def row_pass(scale):
        wide = [jnp.broadcast_to(scale[zz:zz + 1, h * L:(h + 1) * L], (8, L)) for zz in range(Z) for h in range(2)]

        def tile(r, carry):
            rows = pl.ds(pl.multiple_of(r * 32, 32), 32)
            acc = jnp.zeros((4, 8, L), F32)
            for zz in range(Z):
                for h in range(2):
                    acc = acc + K[zz, rows, h * L:(h + 1) * L].reshape(4, 8, L) * wide[zz * 2 + h][None]
            part[rows] = acc.reshape(32, L)
            return carry

        lax.fori_loop(0, CR // 32, tile, 0)

    def col_pass(k):
        def tile(r, accs):
            rows = pl.ds(pl.multiple_of(r * 32, 32), 32)
            w = cwb[rows].reshape(4, 8, L)
            return tuple(
                accs[zz * 2 + h] + jnp.sum(K[zz, rows, h * L:(h + 1) * L].reshape(4, 8, L) * w, axis=0)
                for zz in range(Z)
                for h in range(2)
            )

        accs = lax.fori_loop(0, CR // 32, tile, (jnp.zeros((8, L), F32),) * (2 * Z))
        for zz in range(Z):
            for h in range(2):
                col[k, zz:zz + 1, h * L:(h + 1) * L] = jnp.sum(accs[zz * 2 + h], axis=0, keepdims=True)

    for k in range(SWEEPS):
        if k > 0:
            col_pass(k)
            exchange(col.at[k], colr.at[k], z_targets, k)
        arrive(colr.at[k], k)
        total = col[k]
        for i in range(len(z_offs)):
            total = total + colr[k, i]
        scale = 1.0 / total
        row_pass(scale)
        mine, slots = (row0, row0r) if k == 0 else (row.at[k - 1], rowr.at[k - 1])
        to_lanes(mine, 0)
        exchange(mine, slots, xyc_targets, SWEEPS + k)
        arrive(slots, SWEEPS + k)
        total = mine[...]
        for i in range(len(xyc_offs)):
            total = total + slots[i]
        to_rows(cwb, 1.0 / total[:NB])
        if k == 0:
            to_rows(ltb, jnp.log(total[NB:]))

    cscale[...] = scale

    def gradient_block(zz, loss):
        cs = cscale[pl.ds(zz, 1)]

        def tile(b, loss):
            rows = pl.ds(pl.multiple_of(b * B, B), B)
            w, lt = cwb[rows], ltb[rows]
            w = jnp.concatenate([w, w], axis=1)
            lt = jnp.concatenate([lt, lt], axis=1)
            assign = K[zz, rows] * w * cs
            shifted = S[zz, rows] * 10.0 - lt
            e = jnp.exp2(shifted * LOG2E)
            G[zz, rows] = ((e - assign) * 1024.0).astype(BF16)
            return loss + jnp.sum((assign * shifted).reshape(B // 8, 8, B), axis=0)

        loss = lax.fori_loop(0, NB, tile, loss)

        def contract(b, carry):
            pg[zz] += jnp.dot(UT[b], G[zz, pl.ds(pl.multiple_of(b * B, B), B)], preferred_element_type=F32)
            return carry

        pg[zz] = jnp.zeros((D, B), F32)
        lax.fori_loop(0, NB, contract, 0)
        return loss

    def zi(d):
        return lax.rem(z + d, Z)

    steps = []

    def reduce_step(s):
        if s > 1:
            d = H - s + 1
            for way, zz in ((0, zi(d)), (1, zi(Z - d))):
                steps[-1][way].wait_recv()
                if s == 2:
                    rows = (lo, hi)[way]
                    pg[zz, rows] += pgr[way, 0, rows]
                else:
                    pg[zz] += pgr[way, s - 2]
        if s <= H:
            d = H - s + 1
            if s == 1:
                steps.append((send(pg.at[zi(H), lo], pgr.at[0, 0, lo], up), send(pg.at[zi(H), hi], pgr.at[1, 0, hi], down)))
            else:
                steps.append((send(pg.at[zi(d)], pgr.at[0, s - 1], up), send(pg.at[zi(Z - d)], pgr.at[1, s - 1], down)))

    loss = gradient_block(zi(H), jnp.zeros((8, B), F32))
    reduce_step(1)
    for d in range(H - 1, 0, -1):
        loss = gradient_block(zi(d), loss)
        loss = gradient_block(zi(Z - d), loss)
        if d == max(H - 2, 1):
            reduce_step(2)
    loss = gradient_block(z, loss)

    lz[...] = loss[:, :L] + loss[:, L:]
    exchange(lz, lzr, z_targets, 2 * SWEEPS)

    def crop_block(b):
        acc = jnp.dot(G[0, pl.ds(pl.multiple_of(b * B, B), B)], PR[0], preferred_element_type=F32)
        for zz in range(1, Z):
            acc = acc + jnp.dot(G[zz, pl.ds(pl.multiple_of(b * B, B), B)], PR[zz], preferred_element_type=F32)
        gu[b] = acc

    x_order = [*x_offs, 0]
    core_copies = []
    for d in x_order:
        b = lax.rem(x + d, X) * C + (1 - c)
        crop_block(b)
        core_copies.append(send(gu.at[b], corer.at[lax.rem(x + d, X)], partner))
    reduce_step(3)
    scattered = []
    for d, copy in zip(x_order, core_copies):
        xx = lax.rem(x + d, X)
        b = xx * C + c
        crop_block(b)
        copy.wait_recv()
        gu[b] += corer[xx]
        for i, (ox, oy) in enumerate(xy_offs):
            if ox == d:
                q = pl.ds(pl.multiple_of(lax.rem(y + oy, Y) * Q, Q), Q)
                scattered.append(send(gu.at[b, q], rsr.at[i], at_xyc((ox, oy, 0))))
    arrive(lzr, 2 * SWEEPS)
    total = lz[...]
    for i in range(len(z_offs)):
        total = total + lzr[i]
    lx[...] = total
    exchange(lx, lxr, xyc_targets, 2 * SWEEPS + 1)
    reduce_step(4)
    for copy in scattered:
        copy.wait_recv()
    mine = pl.ds(pl.multiple_of(y * Q, Q), Q)
    total = gu[own, mine]
    for i in range(len(xy_offs)):
        total = total + rsr[i]
    gsb[mine] = unit_back(sf[mine].astype(F32), total)
    y_copies = [send(gsb.at[mine], gsb.at[mine], at_xyc((0, d, 0))) for d in sorted(range(1, Y), key=lambda d: -ring_distance(d, Y))]

    arrive(lxr, 2 * SWEEPS + 1)
    total = lx[...]
    for i in range(len(xyc_offs)):
        total = total + lxr[i]
    loss_o[...] = total

    for way in range(2):
        steps[-1][way].wait_recv()
    rows_sum = (pg[z] + pgr[0, H - 1] + pgr[1, H - 1]).T
    gp_o[...] = unit_back(pw[...], rows_sum)
    for copy in y_copies:
        copy.wait_recv()
    gs_o[...] = gsb[...]

    for copy in sent:
        copy.wait_send()
    for k in range(SWEEPS):
        wait_bytes(colr.at[k], xsem.at[k])
    wait_bytes(row0r, xsem.at[SWEEPS])
    for k in range(1, SWEEPS):
        wait_bytes(rowr.at[k - 1], xsem.at[SWEEPS + k])
    wait_bytes(lzr, xsem.at[2 * SWEEPS])
    wait_bytes(lxr, xsem.at[2 * SWEEPS + 1])


def shards(Z, student_feat, teacher_feat, proto_weight):
    H = Z // 2
    nx, nz = X * Y * C - 1, Z - 1
    vmem = pl.BlockSpec(memory_space=pltpu.VMEM)
    v = pltpu.VMEM
    copies = 256
    gs, gp, loss = pl.pallas_call(
        functools.partial(kernel, Z),
        out_shape=(
            jax.ShapeDtypeStruct((B, D), F32),
            jax.ShapeDtypeStruct((B, D), F32),
            jax.ShapeDtypeStruct((8, L), F32),
        ),
        in_specs=[vmem] * 3,
        out_specs=(vmem,) * 3,
        scratch_shapes=[
            v((NB, B, D), BF16), v((NB, B, D), BF16), v((Z, B, D), BF16),
            v((Z, CR, B), F32), v((Z, CR, B), F32), v((Z, CR, B), BF16), v((NB, D, B), BF16),
            v((CR, L), F32), v((CR, L), F32), v((CR, L), F32),
            v((SWEEPS, Z, B), F32), v((SWEEPS, nz, Z, B), F32),
            v((2 * NB, B), F32), v((nx, 2 * NB, B), F32),
            v((SWEEPS - 1, NB, B), F32), v((SWEEPS - 1, nx, NB, B), F32),
            v((Z, D, B), F32), v((2, H, D, B), F32), v((NB, B, D), F32), v((X, B, D), F32),
            v((X * Y - 1, Q, D), F32), v((B, D), F32),
            v((8, L), F32), v((nz, 8, L), F32), v((8, L), F32), v((nx, 8, L), F32), v((Z, B), F32),
            pltpu.SemaphoreType.DMA((copies,)), pltpu.SemaphoreType.DMA((copies,)),
            pltpu.SemaphoreType.DMA((2 * SWEEPS + 2,)), pltpu.SemaphoreType.DMA((2 * SWEEPS + 2,)),
        ],
        compiler_params=pltpu.CompilerParams(
            collective_id=0, has_side_effects=True, vmem_limit_bytes=62 * 2**20
        ),
        cost_estimate=pl.CostEstimate(flops=8 * CR * Z * B * D, bytes_accessed=2**21, transcendentals=2 * CR * Z * B),
    )(student_feat, teacher_feat, proto_weight)
    crops = NB * Z * B
    return gs, gp, -jnp.sum(loss) / crops


def solution(mesh):
    Z = mesh.shape["dp"] // (X * C)
    return jax.shard_map(
        functools.partial(shards, Z),
        mesh=mesh,
        in_specs=(P("dp", None), P("dp", None), P(("proto", "dp"), None)),
        out_specs=(P("dp", None), P(("proto", "dp"), None), P()),
        check_vma=False,
    )
```

time: 999 us -> 141 us (0.14); the launches traced: 987 us -> 141 us
  waiting for transfers between devices: 714 us -> 0 us
  Pallas kernels: 0 us -> 135 us
  matrix products: 127 us -> 0 us
  blocking collectives: 102 us -> 0 us
  other arithmetic: 25.2 us -> 1.29 us
  between operations: 16.2 us -> 2.43 us
    psum x4 -> x0, waiting for transfers between devices: 483 us -> none  [the longest x3 483 us: by_weights(): lax.psum(jnp.dot(crop_weight, teach_exp, precision=precise), 'dp')]
    reduce_scatter x1 -> x0, waiting for transfers between devices: 144 us -> none  [by_weights(): lax.psum_scatter(lax.dot_general(gradient, student_unit, contract_first,...]
    pallas_call x0 -> x1, Pallas kernels: none -> 135 us  [shards(): pl.pallas_call(functools.partial(kernel, Z), out_shape=(jax.ShapeDtypeStr...]
    dot_general x10 -> x0, matrix products: 127 us -> none  [the longest x3 48.2 us: by_weights(): row_part = jnp.dot(teach_exp, column_scale, precision=precise)]
    psum x4 -> x0, blocking collectives: 102 us -> none  [the longest x1 75.3 us: by_weights(): loss_sum = lax.psum(loss_part, ('dp', 'proto'))]
    all_gather x1 -> x0, waiting for transfers between devices: 87.5 us -> none  [by_weights(): protos = lax.all_gather(proto_unit, 'dp', axis=0, tiled=True)]
    reduce_sum x6 -> x1, other arithmetic: 17.3 us -> 1.29 us  [shards(): return (gs, gp, -jnp.sum(loss) / crops)]
  transfers between devices with their start and end apart: 6 -> 0, of which waited for: 5 -> 0; matrix products, arithmetic and copies ran while one was open for 3% -> 0% of each run, Pallas kernels for 0% -> 0%
where the time goes in v1:
time: 141 us
  Pallas kernels  135 us (96%)
  between operations  2.43 us (2%)
  local copies, waits for them, and re-layouts  2.42 us (2%)
    pallas_call x1, Pallas kernels, shards(): pl.pallas_call(functools.partial(kernel, Z), out_shape=(jax.ShapeDtypeStr...  135 us

profile of v1, /device:TPU:1, one launch (start us, length us, event | category | flops | bytes accessed | tf_op | source)
XLA Modules:
  0.0 140.7 jit_solution(11376083801718184441)
XLA Ops:
  0.6 134.5 %shard_map.58 = (f32[256,256]{1,0:T(8,128)}, f32[256,256]{1,0:T(8,128)}, f32[8,128]{1,0:T(8,128)}) custom-call(bf16[256,256]{1,0:T(8,128)(2,1)} %sf.1, bf16[256,256]{1,0:T(8,128)(2,1)} %tf.1, f32[256,256]{1,0:T(8,128)} %pw.1), custom_call_target="tpu_custom_call" | custom-call | flops 8589934592 | bytes 2097152 | tf_op jit(solution)/shard_map/pallas_call | solution.py:382
  135.2 1.3 reduce_sum.9
  137.1 0.0 copy-start
  137.1 1.7 %copy.8 = f32[256,256]{1,0:T(8,128)} copy(f32[256,256]{1,0:T(8,128)} %get-tuple-element.12) | data formatting | bytes 524288
  138.8 0.0 copy-done
  138.8 0.7 copy.9
Async XLA Ops:
  137.1 1.7 %copy-start = (f32[256,256]{1,0:T(8,128)S(1)}, f32[256,256]{1,0:T(8,128)}, u32[]{:S(2)}) copy-start(f32[256,256]{1,0:T(8,128)} %get-tuple-element.13) | copy-start | bytes 786436

commit v2 on v1

v2 whole, which is shorter than its diff:
```python
import functools
import itertools

import jax
import jax.numpy as jnp
from jax import lax
from jax.experimental import pallas as pl
from jax.experimental.pallas import tpu as pltpu
from jax.sharding import PartitionSpec as P

SWEEPS = 3
X, Y, C = 4, 4, 2
B = 256
D = 256
L = 128
NB = X * C
CR = NB * B
Q = B // Y
NP = 4
SCALE = 1024.0
LOG2E = 1.4426950408889634
EPS = 1e-6
F32, BF16 = jnp.float32, jnp.bfloat16
MESH = pl.DeviceIdType.MESH
NT = (((1,), (1,)), ((), ()))


def inverse_norm(v):
    return lax.rsqrt(jnp.sum(v * v, axis=1, keepdims=True) + EPS)


def unit_back(v, upstream):
    inv = inverse_norm(v)
    u = v * inv
    return (upstream - u * jnp.sum(u * upstream, axis=1, keepdims=True)) * inv


def ring_distance(d, n):
    return min(d, n - d)


def offsets(sizes):
    every = [o for o in itertools.product(*[range(n) for n in sizes]) if any(o)]
    return sorted(every, key=lambda o: -sum(ring_distance(d, n) for d, n in zip(o, sizes)))


def kernel(Z, sf, tf, pw, gs_o, gp_o, loss_o, T, U, PR, K, S, G, cwb, ltb, part, col, colr, stud, studr, row, rowr,
           pg, near, nearr, nxt, nxtr, pgr, corer, rss, rsr, gsb, lz, lzr, lx, lxr, cscale, ssem, rsem, csem, xsem):
    H = Z // 2
    dp, y = lax.axis_index("dp"), lax.axis_index("proto")
    z, x, c = dp // (X * C), lax.rem(dp // C, X), lax.rem(dp, C)

    def dev(zz, xx, yy, cc):
        return ((zz * X + xx) * C + cc, yy)

    def at_z(d):
        return dev(lax.rem(z + d, Z), x, y, c)

    def at_xyc(o):
        return dev(z, lax.rem(x + o[0], X), lax.rem(y + o[1], Y), lax.rem(c + o[2], C))

    z_offs = [o[0] for o in offsets((Z,))]
    xyc_offs = offsets((X, Y, C))
    xy_offs = offsets((X, Y))
    partner = at_xyc((0, 0, 1))

    barrier = pltpu.get_barrier_semaphore()
    for d in z_offs:
        pl.semaphore_signal(barrier, 1, device_id=at_z(d), device_id_type=MESH)
    for o in xyc_offs:
        pl.semaphore_signal(barrier, 1, device_id=at_xyc(o), device_id_type=MESH)

    own = x * C + c
    pv = pw[...]
    PR[z] = (pv * inverse_norm(pv)).astype(BF16)
    tv = tf[...].astype(F32)
    T[own] = (tv * inverse_norm(tv)).astype(BF16)
    sv = sf[...].astype(F32)
    U[own] = (sv * inverse_norm(sv)).astype(BF16)
    pl.semaphore_wait(barrier, len(z_offs) + len(xyc_offs))

    count = [0]
    sent = []

    def send(src, dst, device):
        i = count[0]
        count[0] += 1
        copy = pltpu.make_async_remote_copy(src, dst, ssem.at[i], rsem.at[i], device_id=device, device_id_type=MESH)
        copy.start()
        sent.append(copy)
        return copy

    def wait_bytes(ref, sem):
        pltpu.make_async_copy(ref, ref, sem).wait()

    def exchange(src, slots, targets, k):
        for i, device in enumerate(targets):
            pltpu.make_async_remote_copy(
                src, slots.at[i], xsem.at[k], csem.at[k], device_id=device, device_id_type=MESH
            ).start()

    def arrive(slots, k):
        wait_bytes(slots, csem.at[k])

    z_targets = [at_z(d) for d in z_offs]
    xyc_targets = [at_xyc(o) for o in xyc_offs]

    up, down = at_z(1), at_z(Z - 1)
    half = B // 2
    lo, hi = pl.ds(0, half), pl.ds(half, half)
    pieces = [pl.ds(i * (B // NP), B // NP) for i in range(NP)]
    ring = [[[send(PR.at[z, rows], PR.at[z, rows], way) for rows in pieces] for way in (up, down)]]

    x_offs = sorted(range(1, X), key=lambda d: -ring_distance(d, X))

    def spread(A):
        return [send(A.at[own], A.at[own], at_xyc((d, 0, 0))) for d in x_offs], [send(A.at[own], A.at[own], partner)]

    def pass_on(A, copies):
        got, to_partner = copies
        for d, copy in zip(x_offs, got):
            copy.wait_recv()
            b = lax.rem(x + X - d, X) * C + c
            to_partner.append(send(A.at[b], A.at[b], partner))

    t_copies = spread(T)

    def ring_step(s):
        step = [[None] * NP, [None] * NP]
        for i, rows in enumerate(pieces):
            for w, (zz, way) in enumerate(((lax.rem(z + Z - s, Z), up), (lax.rem(z + s, Z), down))):
                if ring[s - 1][w][i] is not None:
                    ring[s - 1][w][i].wait_recv()
                    if s + 1 < H or (s < H and (i < NP // 2) == (w == 0)):
                        step[w][i] = send(PR.at[zz, rows], PR.at[zz, rows], way)
        ring.append(step)

    def teacher_block(zz):
        protos = PR[zz]

        def tile(b, acc):
            logits = lax.dot_general(T[b], protos, NT, preferred_element_type=F32)
            e = jnp.exp2(logits * (25.0 * LOG2E))
            K[zz, pl.ds(pl.multiple_of(b * B, B), B)] = e
            return acc + jnp.sum(e.reshape(B // 8, 8, B), axis=0)

        acc = lax.fori_loop(0, NB, tile, jnp.zeros((8, B), F32), unroll=NB)
        col[0, pl.ds(zz, 1)] = jnp.sum(acc, axis=0, keepdims=True)

    ring_step(1)
    pass_on(T, t_copies)
    u_copies = spread(U)
    for s in range(2, H):
        ring_step(s)
        if s == 2:
            for copy in t_copies[1]:
                copy.wait_recv()
            teacher_block(z)
        else:
            pass_on(U, u_copies)
        teacher_block(lax.rem(z + Z - s + 1, Z))
        teacher_block(lax.rem(z + s - 1, Z))
    ring_step(H)
    teacher_block(lax.rem(z + Z - H + 1, Z))
    teacher_block(lax.rem(z + H - 1, Z))
    teacher_block(lax.rem(z + H, Z))
    exchange(col.at[0], colr.at[0], z_targets, 0)

    for copy in u_copies[1]:
        copy.wait_recv()

    part[...] = jnp.zeros_like(part)

    def student_block(zz, carry):
        protos = PR[zz]

        def tile(b, carry):
            rows = pl.ds(pl.multiple_of(b * B, B), B)
            scores = lax.dot_general(U[b], protos, NT, preferred_element_type=F32) * (10.0 * LOG2E)
            S[zz, rows] = scores
            e = jnp.exp2(scores)
            part[rows] += e[:, :L] + e[:, L:]
            return carry

        return lax.fori_loop(0, NB, tile, carry, unroll=NB)

    lax.fori_loop(0, Z, student_block, 0)
    used = t_copies[0] + t_copies[1]
    for copy in used:
        copy.wait_send()
    sent[:] = [copy for copy in sent if all(copy is not other for other in used)]
    UT = T
    for b in range(NB):
        UT[b] = U[b].T

    def to_lanes(dst):
        for b in range(NB):
            dst[b:b + 1, :] = jnp.sum(part[b * B:(b + 1) * B].T, axis=0, keepdims=True)

    def to_rows(dst, values):
        for b in range(NB):
            dst[b * B:(b + 1) * B, :] = jnp.broadcast_to(values[b:b + 1], (L, B)).T

    to_lanes(stud)

    R = 128

    def row_pass(scale):
        wide = [jnp.broadcast_to(scale[zz:zz + 1, h * L:(h + 1) * L], (8, L)) for zz in range(Z) for h in range(2)]

        def tile(r, carry):
            rows = pl.ds(pl.multiple_of(r * R, R), R)
            acc = jnp.zeros((R // 8, 8, L), F32)
            for zz in range(Z):
                for h in range(2):
                    acc = acc + K[zz, rows, h * L:(h + 1) * L].reshape(R // 8, 8, L) * wide[zz * 2 + h][None]
            part[rows] = acc.reshape(R, L)
            return carry

        lax.fori_loop(0, CR // R, tile, 0, unroll=2)

    def col_pass(k):
        def tile(r, accs):
            rows = pl.ds(pl.multiple_of(r * R, R), R)
            w = cwb[rows].reshape(R // 8, 8, L)
            return tuple(
                accs[zz * 2 + h] + jnp.sum(K[zz, rows, h * L:(h + 1) * L].reshape(R // 8, 8, L) * w, axis=0)
                for zz in range(Z)
                for h in range(2)
            )

        accs = lax.fori_loop(0, CR // R, tile, (jnp.zeros((8, L), F32),) * (2 * Z), unroll=2)
        for zz in range(Z):
            for h in range(2):
                col[k, zz:zz + 1, h * L:(h + 1) * L] = jnp.sum(accs[zz * 2 + h], axis=0, keepdims=True)

    for k in range(SWEEPS):
        if k > 0:
            col_pass(k)
            exchange(col.at[k], colr.at[k], z_targets, k)
        arrive(colr.at[k], k)
        total = col[k]
        for i in range(len(z_offs)):
            total = total + colr[k, i]
        scale = 1.0 / total
        row_pass(scale)
        mine, slots = row.at[k], rowr.at[k]
        to_lanes(mine)
        exchange(mine, slots, xyc_targets, SWEEPS + k)
        if k == 0:
            exchange(stud, studr, xyc_targets, 2 * SWEEPS + 2)
        arrive(slots, SWEEPS + k)
        total = mine[...]
        for i in range(len(xyc_offs)):
            total = total + slots[i]
        to_rows(cwb, 1.0 / total)
        if k == 1:
            arrive(studr, 2 * SWEEPS + 2)
            total = stud[...]
            for i in range(len(xyc_offs)):
                total = total + studr[i]
            to_rows(ltb, jnp.log(total) * LOG2E)

    cscale[...] = scale

    def gradient_block(zz, loss):
        cs = cscale[pl.ds(zz, 1)]

        acc = jnp.zeros((D, B), F32)
        for b in range(NB):
            rows = slice(b * B, (b + 1) * B)
            w, lt = cwb[rows], ltb[rows]
            w = jnp.concatenate([w, w], axis=1)
            lt = jnp.concatenate([lt, lt], axis=1)
            assign = K[zz, rows] * w * cs
            shifted = S[zz, rows] - lt
            g = (jnp.exp2(shifted) - assign).astype(BF16)
            G[zz, rows] = g
            loss = loss + jnp.sum((assign * shifted).reshape(B // 8, 8, B), axis=0)
            acc = acc + jnp.dot(UT[b], g, preferred_element_type=F32)
        pg[zz] = acc
        return loss

    def zi(d):
        return lax.rem(z + d, Z)

    steps = []

    def reduce_step(s):
        d = H - s + 1
        step = [[], []]
        for i, rows in enumerate((lo, hi)):
            for w, (zz, way) in enumerate(((zi(d), up), (zi(Z - d), down))):
                if s == 1:
                    if i == w:
                        near[w, rows] = pg[zz, rows].astype(BF16)
                        step[w].append(send(near.at[w, rows], nearr.at[w, rows], way))
                elif s == 2:
                    total = pg[zz, rows]
                    if i == w:
                        steps[-1][w][0].wait_recv()
                        total = total + nearr[w, rows].astype(F32)
                    nxt[w, rows] = total.astype(BF16)
                    step[w].append(send(nxt.at[w, rows], nxtr.at[w, rows], way))
                else:
                    steps[-1][w][i].wait_recv()
                    came = nxtr[w, rows].astype(F32) if s == 3 else pgr[w, s - 4, rows]
                    pg[zz, rows] += came
                    if s <= H:
                        step[w].append(send(pg.at[zz, rows], pgr.at[w, s - 3, rows], way))
        steps.append(step)

    loss = gradient_block(zi(H), jnp.zeros((8, B), F32))
    reduce_step(1)
    for d in range(H - 1, 0, -1):
        loss = gradient_block(zi(d), loss)
        loss = gradient_block(zi(Z - d), loss)
        if d == H - 2:
            reduce_step(2)
    loss = gradient_block(z, loss)

    lz[...] = loss[:, :L] + loss[:, L:]
    exchange(lz, lzr, z_targets, 2 * SWEEPS)

    def gu(b, first=0, n=B):
        return K.at[0, pl.ds(pl.multiple_of(b * B + first, n), n)]

    def crop_block(b):
        acc = jnp.dot(G[0, pl.ds(pl.multiple_of(b * B, B), B)], PR[0], preferred_element_type=F32)
        for zz in range(1, Z):
            acc = acc + jnp.dot(G[zz, pl.ds(pl.multiple_of(b * B, B), B)], PR[zz], preferred_element_type=F32)
        gu(b)[...] = acc

    x_order = [*x_offs, 0]
    core_copies = []
    for d in x_order:
        b = lax.rem(x + d, X) * C + (1 - c)
        crop_block(b)
        core_copies.append(send(gu(b), corer.at[lax.rem(x + d, X)], partner))
    reduce_step(3)
    scattered = []
    for d, copy in zip(x_order, core_copies):
        xx = lax.rem(x + d, X)
        b = xx * C + c
        crop_block(b)
        copy.wait_recv()
        total = gu(b)[...] + corer[xx]
        gu(b)[...] = total
        rss[xx] = total.astype(BF16)
        for i, (ox, oy) in enumerate(xy_offs):
            if ox == d:
                q = pl.ds(pl.multiple_of(lax.rem(y + oy, Y) * Q, Q), Q)
                scattered.append(send(rss.at[xx, q], rsr.at[i], at_xyc((ox, oy, 0))))
    arrive(lzr, 2 * SWEEPS)
    total = lz[...]
    for i in range(len(z_offs)):
        total = total + lzr[i]
    lx[...] = total
    exchange(lx, lxr, xyc_targets, 2 * SWEEPS + 1)
    reduce_step(4)
    for copy in scattered:
        copy.wait_recv()
    mine = pl.ds(pl.multiple_of(y * Q, Q), Q)
    total = gu(own, y * Q, Q)[...]
    for i in range(len(xy_offs)):
        total = total + rsr[i].astype(F32)
    gsb[mine] = total
    y_copies = [send(gsb.at[mine], gsb.at[mine], at_xyc((0, d, 0))) for d in sorted(range(1, Y), key=lambda d: -ring_distance(d, Y))]

    arrive(lxr, 2 * SWEEPS + 1)
    total = lx[...]
    for i in range(len(xyc_offs)):
        total = total + lxr[i]
    loss_o[...] = total

    reduce_step(H + 1)
    gp_o[...] = pg[z].T
    for copy in y_copies:
        copy.wait_recv()
    gs_o[...] = gsb[...]

    for copy in sent:
        copy.wait_send()
    for k in range(SWEEPS):
        wait_bytes(colr.at[k], xsem.at[k])
        wait_bytes(rowr.at[k], xsem.at[SWEEPS + k])
    wait_bytes(studr, xsem.at[2 * SWEEPS + 2])
    wait_bytes(lzr, xsem.at[2 * SWEEPS])
    wait_bytes(lxr, xsem.at[2 * SWEEPS + 1])


def finish(crops, sf, pw, gs, gp, loss, gs_o, gp_o, loss_o):
    gs_o[...] = unit_back(sf[...].astype(F32), gs[...] * SCALE)
    gp_o[...] = unit_back(pw[...], gp[...] * SCALE)
    loss_o[0, 0] = jnp.sum(loss[...]) * (-1.0 / (LOG2E * crops))


def shards(Z, student_feat, teacher_feat, proto_weight):
    H = Z // 2
    nx, nz = X * Y * C - 1, Z - 1
    vmem = pl.BlockSpec(memory_space=pltpu.VMEM)
    v = pltpu.VMEM
    copies = 256
    gs, gp, loss = pl.pallas_call(
        functools.partial(kernel, Z),
        out_shape=(
            jax.ShapeDtypeStruct((B, D), F32),
            jax.ShapeDtypeStruct((B, D), F32),
            jax.ShapeDtypeStruct((8, L), F32),
        ),
        in_specs=[vmem] * 3,
        out_specs=(vmem,) * 3,
        scratch_shapes=[
            v((NB, B, D), BF16), v((NB, B, D), BF16), v((Z, B, D), BF16),
            v((Z, CR, B), F32), v((Z, CR, B), F32), v((Z, CR, B), BF16),
            v((CR, L), F32), v((CR, L), F32), v((CR, L), F32),
            v((SWEEPS, Z, B), F32), v((SWEEPS, nz, Z, B), F32),
            v((NB, B), F32), v((nx, NB, B), F32),
            v((SWEEPS, NB, B), F32), v((SWEEPS, nx, NB, B), F32),
            v((Z, D, B), F32), v((2, D, B), BF16), v((2, D, B), BF16), v((2, D, B), BF16), v((2, D, B), BF16),
            v((2, H - 2, D, B), F32), v((X, B, D), F32), v((X, B, D), BF16),
            v((X * Y - 1, Q, D), BF16), v((B, D), F32),
            v((8, L), F32), v((nz, 8, L), F32), v((8, L), F32), v((nx, 8, L), F32), v((Z, B), F32),
            pltpu.SemaphoreType.DMA((copies,)), pltpu.SemaphoreType.DMA((copies,)),
            pltpu.SemaphoreType.DMA((2 * SWEEPS + 3,)), pltpu.SemaphoreType.DMA((2 * SWEEPS + 3,)),
        ],
        compiler_params=pltpu.CompilerParams(
            collective_id=0, has_side_effects=True, vmem_limit_bytes=62 * 2**20
        ),
        cost_estimate=pl.CostEstimate(flops=8 * CR * Z * B * D, bytes_accessed=2**21, transcendentals=2 * CR * Z * B),
    )(student_feat, teacher_feat, proto_weight)
    gs, gp, loss = pl.pallas_call(
        functools.partial(finish, NB * Z * B),
        out_shape=(
            jax.ShapeDtypeStruct((B, D), F32),
            jax.ShapeDtypeStruct((B, D), F32),
            jax.ShapeDtypeStruct((1, 1), F32),
        ),
        in_specs=[vmem] * 5,
        out_specs=(vmem, vmem, pl.BlockSpec(memory_space=pltpu.SMEM)),
    )(student_feat, proto_weight, gs, gp, loss)
    return gs, gp, loss.reshape(())


def solution(mesh):
    Z = mesh.shape["dp"] // (X * C)
    return jax.shard_map(
        functools.partial(shards, Z),
        mesh=mesh,
        in_specs=(P("dp", None), P("dp", None), P(("proto", "dp"), None)),
        out_specs=(P("dp", None), P(("proto", "dp"), None), P()),
        check_vma=False,
    )
```

time: 141 us -> 101 us (0.72)
  Pallas kernels: 135 us -> 99.8 us
  local copies, waits for them, and re-layouts: 2.42 us -> 0 us
  between operations: 2.43 us -> 0.8 us
    pallas_call x1, Pallas kernels: 135 us -> 97.6 us  [shards(): pl.pallas_call(functools.partial(kernel, Z), out_shape=(jax.ShapeDtypeStr...]
    unnamed x4 -> x0, local copies, waits for them, and re-layouts: 2.42 us -> none
    pallas_call x0 -> x1, Pallas kernels: none -> 2.17 us  [shards(): pl.pallas_call(functools.partial(finish, NB * Z * B), out_shape=(jax.Shap...]
where the time goes in v2:
time: 101 us
  Pallas kernels  99.8 us (99%)
    pallas_call x1, Pallas kernels, shards(): pl.pallas_call(functools.partial(kernel, Z), out_shape=(jax.ShapeDtypeStr...  97.6 us
    pallas_call x1, Pallas kernels, shards(): pl.pallas_call(functools.partial(finish, NB * Z * B), out_shape=(jax.Shap...  2.17 us

profile of v2, /device:TPU:1, one launch (start us, length us, event | category | flops | bytes accessed | tf_op | source)
XLA Modules:
  0.0 100.6 jit_solution(6740422884627586192)
XLA Ops:
  0.6 97.6 %shard_map.58 = (f32[256,256]{1,0:T(8,128)}, f32[256,256]{1,0:T(8,128)}, f32[8,128]{1,0:T(8,128)}) custom-call(bf16[256,256]{1,0:T(8,128)(2,1)} %sf.3, bf16[256,256]{1,0:T(8,128)(2,1)} %tf.1, f32[256,256]{1,0:T(8,128)} %pw.3), custom_call_target="tpu_custom_call" | custom-call | flops 8589934592 | bytes 2097152 | tf_op jit(solution)/shard_map/pallas_call | solution.py:404
  98.2 2.2 %shard_map.59 = (f32[256,256]{1,0:T(8,128)}, f32[256,256]{1,0:T(8,128)}, f32[1,1]{1,0:T(1,128)}) custom-call(bf16[256,256]{1,0:T(8,128)(2,1)} %sf.3, f32[256,256]{1,0:T(8,128)} %pw.3, f32[256,256]{1,0:T(8,128)} %get-tuple-element.9.gs, f32[256,256]{1,0:T(8,128)} %get-tuple-element.10.gp, f32[8,128]{1,0:T(8,128)} %get-tuple-element.11.loss), custom_call_target="tpu_custom_call" | custom-call | tf_op jit(solution)/shard_map/pallas_call | solution.py:432

commit v3 on v2

--- a/solution.py
+++ b/solution.py
@@ -44,9 +44,9 @@
     return sorted(every, key=lambda o: -sum(ring_distance(d, n) for d, n in zip(o, sizes)))
 
 
-def kernel(Z, sf, tf, pw, gs_o, gp_o, loss_o, T, U, PR, K, S, G, cwb, ltb, part, col, colr, stud, studr, row, rowr,
-           pg, near, nearr, nxt, nxtr, pgr, corer, rss, rsr, gsb, lz, lzr, lx, lxr, cscale, ssem, rsem, csem, xsem):
-    H = Z // 2
+def kernel(Z, sf_in, tf_in, pw_in, gs_o, gp_o, loss_o, T, U, PR, K, S, G, cwb, ltb, part, col, colr, stud, studr, wide_row, row, rowr,
+           pg, near, nearr, nxt, nxtr, pgr, corer, rss, rsr, gsb, lz, lzr, lx, lxr, cscale, sf, tf, pw, lsem, ssem, rsem, csem, xsem):
+    H = ZH = Z // 2
     dp, y = lax.axis_index("dp"), lax.axis_index("proto")
     z, x, c = dp // (X * C), lax.rem(dp // C, X), lax.rem(dp, C)
 
@@ -64,6 +64,11 @@
     xy_offs = offsets((X, Y))
     partner = at_xyc((0, 0, 1))
 
+    loads = [
+        pltpu.make_async_copy(src, dst, lsem.at[i]) for i, (src, dst) in enumerate(((pw_in, pw), (tf_in, tf), (sf_in, sf)))
+    ]
+    for load in loads:
+        load.start()
     barrier = pltpu.get_barrier_semaphore()
     for d in z_offs:
         pl.semaphore_signal(barrier, 1, device_id=at_z(d), device_id_type=MESH)
@@ -71,12 +76,13 @@
         pl.semaphore_signal(barrier, 1, device_id=at_xyc(o), device_id_type=MESH)
 
     own = x * C + c
-    pv = pw[...]
-    PR[z] = (pv * inverse_norm(pv)).astype(BF16)
-    tv = tf[...].astype(F32)
-    T[own] = (tv * inverse_norm(tv)).astype(BF16)
-    sv = sf[...].astype(F32)
-    U[own] = (sv * inverse_norm(sv)).astype(BF16)
+
+    def unit_into(dst, load, src):
+        load.wait()
+        v = src[...].astype(F32)
+        dst[...] = (v * inverse_norm(v)).astype(BF16)
+
+    unit_into(PR.at[z], loads[0], pw)
     pl.semaphore_wait(barrier, len(z_offs) + len(xyc_offs))
 
     count = [0]
@@ -123,7 +129,9 @@
             b = lax.rem(x + X - d, X) * C + c
             to_partner.append(send(A.at[b], A.at[b], partner))
 
+    unit_into(T.at[own], loads[1], tf)
     t_copies = spread(T)
+    unit_into(U.at[own], loads[2], sf)
 
     def ring_step(s):
         step = [[None] * NP, [None] * NP]
@@ -145,7 +153,9 @@
             return acc + jnp.sum(e.reshape(B // 8, 8, B), axis=0)
 
         acc = lax.fori_loop(0, NB, tile, jnp.zeros((8, B), F32), unroll=NB)
-        col[0, pl.ds(zz, 1)] = jnp.sum(acc, axis=0, keepdims=True)
+        sums = jnp.sum(acc, axis=0, keepdims=True)
+        for h in range(2):
+            col[0, zz // ZH, pl.ds(lax.rem(zz, ZH) * 2 + h, 1)] = sums[:, h * L:(h + 1) * L]
 
     ring_step(1)
     pass_on(T, t_copies)
@@ -164,7 +174,11 @@
     teacher_block(lax.rem(z + Z - H + 1, Z))
     teacher_block(lax.rem(z + H - 1, Z))
     teacher_block(lax.rem(z + H, Z))
-    exchange(col.at[0], colr.at[0], z_targets, 0)
+    def col_exchange(k, part_of):
+        exchange(col.at[k, part_of], colr.at[k, part_of], z_targets, k + part_of * (2 * SWEEPS + 3))
+
+    col_exchange(0, 0)
+    col_exchange(0, 1)
 
     for copy in u_copies[1]:
         copy.wait_recv()
@@ -195,131 +209,153 @@
 
     def to_lanes(dst):
         for b in range(NB):
-            dst[b:b + 1, :] = jnp.sum(part[b * B:(b + 1) * B].T, axis=0, keepdims=True)
+            sums = jnp.sum(part[b * B:(b + 1) * B].T, axis=0, keepdims=True)
+            for h in range(2):
+                wide_row[h * NB + b:h * NB + b + 1, :] = sums[:, h * L:(h + 1) * L]
+        dst[...] = wide_row[...].astype(BF16)
 
     def to_rows(dst, values):
         for b in range(NB):
-            dst[b * B:(b + 1) * B, :] = jnp.broadcast_to(values[b:b + 1], (L, B)).T
+            for h in range(2):
+                i = h * NB + b
+                dst[b * B + h * L:b * B + (h + 1) * L, :] = jnp.broadcast_to(values[i:i + 1], (L, L)).T
 
     to_lanes(stud)
 
     R = 128
 
-    def row_pass(scale):
-        wide = [jnp.broadcast_to(scale[zz:zz + 1, h * L:(h + 1) * L], (8, L)) for zz in range(Z) for h in range(2)]
+    def row_pass(part_of, scale):
+        wide = [jnp.broadcast_to(scale[i:i + 1], (8, L)) for i in range(2 * ZH)]
 
         def tile(r, carry):
             rows = pl.ds(pl.multiple_of(r * R, R), R)
-            acc = jnp.zeros((R // 8, 8, L), F32)
-            for zz in range(Z):
-                for h in range(2):
-                    acc = acc + K[zz, rows, h * L:(h + 1) * L].reshape(R // 8, 8, L) * wide[zz * 2 + h][None]
+            acc = part[rows].reshape(R // 8, 8, L) if part_of else jnp.zeros((R // 8, 8, L), F32)
+            for i in range(2 * ZH):
+                zz, h = part_of * ZH + i // 2, i % 2
+                acc = acc + K[zz, rows, h * L:(h + 1) * L].reshape(R // 8, 8, L) * wide[i][None]
             part[rows] = acc.reshape(R, L)
             return carry
 
         lax.fori_loop(0, CR // R, tile, 0, unroll=2)
 
-    def col_pass(k):
+    def col_pass(k, part_of):
         def tile(r, accs):
             rows = pl.ds(pl.multiple_of(r * R, R), R)
             w = cwb[rows].reshape(R // 8, 8, L)
             return tuple(
-                accs[zz * 2 + h] + jnp.sum(K[zz, rows, h * L:(h + 1) * L].reshape(R // 8, 8, L) * w, axis=0)
-                for zz in range(Z)
-                for h in range(2)
+                accs[i] + jnp.sum(K[part_of * ZH + i // 2, rows, i % 2 * L:(i % 2 + 1) * L].reshape(R // 8, 8, L) * w, axis=0)
+                for i in range(2 * ZH)
             )
 
-        accs = lax.fori_loop(0, CR // R, tile, (jnp.zeros((8, L), F32),) * (2 * Z), unroll=2)
-        for zz in range(Z):
-            for h in range(2):
-                col[k, zz:zz + 1, h * L:(h + 1) * L] = jnp.sum(accs[zz * 2 + h], axis=0, keepdims=True)
+        accs = lax.fori_loop(0, CR // R, tile, (jnp.zeros((8, L), F32),) * (2 * ZH), unroll=2)
+        for i in range(2 * ZH):
+            col[k, part_of, i:i + 1] = jnp.sum(accs[i], axis=0, keepdims=True)
+
+    def prepare():
+        def tile(b, carry):
+            rows = pl.ds(pl.multiple_of(b * B, B), B)
+            lt = jnp.concatenate([ltb[rows], ltb[rows]], axis=1)
+            acc = jnp.zeros((B, L), F32)
+            for zz in range(Z):
+                shifted = S[zz, rows] - lt
+                S[zz, rows] = jnp.exp2(shifted)
+                weighed = K[zz, rows] * cscale[zz:zz + 1] * shifted
+                acc = acc + weighed[:, :L] + weighed[:, L:]
+            part[rows] = acc
+            return carry
+
+        lax.fori_loop(0, NB, tile, 0)
 
     for k in range(SWEEPS):
         if k > 0:
-            col_pass(k)
-            exchange(col.at[k], colr.at[k], z_targets, k)
-        arrive(colr.at[k], k)
-        total = col[k]
-        for i in range(len(z_offs)):
-            total = total + colr[k, i]
-        scale = 1.0 / total
-        row_pass(scale)
+            for part_of in range(2):
+                col_pass(k, part_of)
+                col_exchange(k, part_of)
+        for part_of in range(2):
+            arrive(colr.at[k, part_of], k + part_of * (2 * SWEEPS + 3))
+            total = col[k, part_of]
+            for i in range(len(z_offs)):
+                total = total + colr[k, part_of, i]
+            scale = 1.0 / total
+            row_pass(part_of, scale)
+            if k == SWEEPS - 1:
+                for i in range(2 * ZH):
+                    zz, h = part_of * ZH + i // 2, i % 2
+                    cscale[zz:zz + 1, h * L:(h + 1) * L] = scale[i:i + 1]
         mine, slots = row.at[k], rowr.at[k]
         to_lanes(mine)
         exchange(mine, slots, xyc_targets, SWEEPS + k)
         if k == 0:
             exchange(stud, studr, xyc_targets, 2 * SWEEPS + 2)
+        if k == SWEEPS - 1:
+            prepare()
         arrive(slots, SWEEPS + k)
-        total = mine[...]
+        total = mine[...].astype(F32)
         for i in range(len(xyc_offs)):
-            total = total + slots[i]
+            total = total + slots[i].astype(F32)
         to_rows(cwb, 1.0 / total)
         if k == 1:
             arrive(studr, 2 * SWEEPS + 2)
-            total = stud[...]
+            total = stud[...].astype(F32)
             for i in range(len(xyc_offs)):
-                total = total + studr[i]
+                total = total + studr[i].astype(F32)
             to_rows(ltb, jnp.log(total) * LOG2E)
 
-    cscale[...] = scale
-
-    def gradient_block(zz, loss):
+
+    def gradient_block(zz):
         cs = cscale[pl.ds(zz, 1)]
 
         acc = jnp.zeros((D, B), F32)
         for b in range(NB):
             rows = slice(b * B, (b + 1) * B)
-            w, lt = cwb[rows], ltb[rows]
-            w = jnp.concatenate([w, w], axis=1)
-            lt = jnp.concatenate([lt, lt], axis=1)
-            assign = K[zz, rows] * w * cs
-            shifted = S[zz, rows] - lt
-            g = (jnp.exp2(shifted) - assign).astype(BF16)
+            w = jnp.concatenate([cwb[rows], cwb[rows]], axis=1)
+            g = (S[zz, rows] - K[zz, rows] * w * cs).astype(BF16)
             G[zz, rows] = g
-            loss = loss + jnp.sum((assign * shifted).reshape(B // 8, 8, B), axis=0)
             acc = acc + jnp.dot(UT[b], g, preferred_element_type=F32)
         pg[zz] = acc
-        return loss
 
     def zi(d):
         return lax.rem(z + d, Z)
 
     steps = []
 
-    def reduce_step(s):
+    def reduce_step(s, j):
         d = H - s + 1
-        step = [[], []]
-        for i, rows in enumerate((lo, hi)):
-            for w, (zz, way) in enumerate(((zi(d), up), (zi(Z - d), down))):
-                if s == 1:
-                    if i == w:
-                        near[w, rows] = pg[zz, rows].astype(BF16)
-                        step[w].append(send(near.at[w, rows], nearr.at[w, rows], way))
-                elif s == 2:
-                    total = pg[zz, rows]
-                    if i == w:
-                        steps[-1][w][0].wait_recv()
-                        total = total + nearr[w, rows].astype(F32)
-                    nxt[w, rows] = total.astype(BF16)
-                    step[w].append(send(nxt.at[w, rows], nxtr.at[w, rows], way))
-                else:
-                    steps[-1][w][i].wait_recv()
-                    came = nxtr[w, rows].astype(F32) if s == 3 else pgr[w, s - 4, rows]
-                    pg[zz, rows] += came
-                    if s <= H:
-                        step[w].append(send(pg.at[zz, rows], pgr.at[w, s - 3, rows], way))
-        steps.append(step)
-
-    loss = gradient_block(zi(H), jnp.zeros((8, B), F32))
-    reduce_step(1)
+        if j == 0:
+            steps.append([[None, None], [None, None]])
+        for w, (zz, way) in enumerate(((zi(d), up), (zi(Z - d), down))):
+            i = w if j else 1 - w
+            rows = (lo, hi)[i]
+            if s == 1:
+                if j:
+                    near[w, rows] = pg[zz, rows].astype(BF16)
+                    steps[-1][w][i] = send(near.at[w, rows], nearr.at[w, rows], way)
+            elif s == 2:
+                total = pg[zz, rows]
+                if j:
+                    steps[-2][w][i].wait_recv()
+                    total = total + nearr[w, rows].astype(F32)
+                nxt[w, rows] = total.astype(BF16)
+                steps[-1][w][i] = send(nxt.at[w, rows], nxtr.at[w, rows], way)
+            else:
+                steps[-2][w][i].wait_recv()
+                came = nxtr[w, rows].astype(F32) if s == 3 else pgr[w, s - 4, rows]
+                pg[zz, rows] += came
+                if s <= H:
+                    steps[-1][w][i] = send(pg.at[zz, rows], pgr.at[w, s - 3, rows], way)
+
+    gradient_block(zi(H))
+    reduce_step(1, 0)
+    reduce_step(1, 1)
     for d in range(H - 1, 0, -1):
-        loss = gradient_block(zi(d), loss)
-        loss = gradient_block(zi(Z - d), loss)
-        if d == H - 2:
-            reduce_step(2)
-    loss = gradient_block(z, loss)
-
-    lz[...] = loss[:, :L] + loss[:, L:]
+        gradient_block(zi(d))
+        gradient_block(zi(Z - d))
+        if d == H - 1:
+            reduce_step(2, 0)
+    gradient_block(z)
+    reduce_step(2, 1)
+
+    lz[...] = jnp.sum((part[...] * cwb[...]).reshape(CR // 8, 8, L), axis=0)
     exchange(lz, lzr, z_targets, 2 * SWEEPS)
 
     def gu(b, first=0, n=B):
@@ -337,7 +373,7 @@
         b = lax.rem(x + d, X) * C + (1 - c)
         crop_block(b)
         core_copies.append(send(gu(b), corer.at[lax.rem(x + d, X)], partner))
-    reduce_step(3)
+    reduce_step(3, 0)
     scattered = []
     for d, copy in zip(x_order, core_copies):
         xx = lax.rem(x + d, X)
@@ -351,13 +387,15 @@
             if ox == d:
                 q = pl.ds(pl.multiple_of(lax.rem(y + oy, Y) * Q, Q), Q)
                 scattered.append(send(rss.at[xx, q], rsr.at[i], at_xyc((ox, oy, 0))))
+    reduce_step(3, 1)
     arrive(lzr, 2 * SWEEPS)
     total = lz[...]
     for i in range(len(z_offs)):
         total = total + lzr[i]
     lx[...] = total
     exchange(lx, lxr, xyc_targets, 2 * SWEEPS + 1)
-    reduce_step(4)
+    reduce_step(4, 0)
+    reduce_step(4, 1)
     for copy in scattered:
         copy.wait_recv()
     mine = pl.ds(pl.multiple_of(y * Q, Q), Q)
@@ -373,7 +411,8 @@
         total = total + lxr[i]
     loss_o[...] = total
 
-    reduce_step(H + 1)
+    reduce_step(H + 1, 0)
+    reduce_step(H + 1, 1)
     gp_o[...] = pg[z].T
     for copy in y_copies:
         copy.wait_recv()
@@ -382,7 +421,8 @@
     for copy in sent:
         copy.wait_send()
     for k in range(SWEEPS):
-        wait_bytes(colr.at[k], xsem.at[k])
+        for part_of in range(2):
+            wait_bytes(colr.at[k, part_of], xsem.at[k + part_of * (2 * SWEEPS + 3)])
         wait_bytes(rowr.at[k], xsem.at[SWEEPS + k])
     wait_bytes(studr, xsem.at[2 * SWEEPS + 2])
     wait_bytes(lzr, xsem.at[2 * SWEEPS])
@@ -408,21 +448,22 @@
             jax.ShapeDtypeStruct((B, D), F32),
             jax.ShapeDtypeStruct((8, L), F32),
         ),
-        in_specs=[vmem] * 3,
+        in_specs=[pl.BlockSpec(memory_space=pl.ANY)] * 3,
         out_specs=(vmem,) * 3,
         scratch_shapes=[
             v((NB, B, D), BF16), v((NB, B, D), BF16), v((Z, B, D), BF16),
             v((Z, CR, B), F32), v((Z, CR, B), F32), v((Z, CR, B), BF16),
             v((CR, L), F32), v((CR, L), F32), v((CR, L), F32),
-            v((SWEEPS, Z, B), F32), v((SWEEPS, nz, Z, B), F32),
-            v((NB, B), F32), v((nx, NB, B), F32),
-            v((SWEEPS, NB, B), F32), v((SWEEPS, nx, NB, B), F32),
+            v((SWEEPS, 2, Z, L), F32), v((SWEEPS, 2, nz, Z, L), F32),
+            v((2 * NB, L), BF16), v((nx, 2 * NB, L), BF16), v((2 * NB, L), F32),
+            v((SWEEPS, 2 * NB, L), BF16), v((SWEEPS, nx, 2 * NB, L), BF16),
             v((Z, D, B), F32), v((2, D, B), BF16), v((2, D, B), BF16), v((2, D, B), BF16), v((2, D, B), BF16),
             v((2, H - 2, D, B), F32), v((X, B, D), F32), v((X, B, D), BF16),
             v((X * Y - 1, Q, D), BF16), v((B, D), F32),
             v((8, L), F32), v((nz, 8, L), F32), v((8, L), F32), v((nx, 8, L), F32), v((Z, B), F32),
+            v((B, D), BF16), v((B, D), BF16), v((B, D), F32), pltpu.SemaphoreType.DMA((3,)),
             pltpu.SemaphoreType.DMA((copies,)), pltpu.SemaphoreType.DMA((copies,)),
-            pltpu.SemaphoreType.DMA((2 * SWEEPS + 3,)), pltpu.SemaphoreType.DMA((2 * SWEEPS + 3,)),
+            pltpu.SemaphoreType.DMA((3 * SWEEPS + 3,)), pltpu.SemaphoreType.DMA((3 * SWEEPS + 3,)),
         ],
         compiler_params=pltpu.CompilerParams(
             collective_id=0, has_side_effects=True, vmem_limit_bytes=62 * 2**20

time: 101 us -> 95.8 us (0.949)
  Pallas kernels: 99.8 us -> 94.9 us
    pallas_call x1, Pallas kernels: 97.6 us -> 92.7 us  [shards(): pl.pallas_call(functools.partial(kernel, Z), out_shape=(jax.ShapeDtypeStr...]
where the time goes in v3:
time: 95.8 us; the launch traced here: 95.7 us
  Pallas kernels  94.9 us (99%)
    pallas_call x1, Pallas kernels, shards(): pl.pallas_call(functools.partial(kernel, Z), out_shape=(jax.ShapeDtypeStr...  92.7 us
    pallas_call x1, Pallas kernels, shards(): pl.pallas_call(functools.partial(finish, NB * Z * B), out_shape=(jax.Shap...  2.17 us

profile of v3, /device:TPU:1, one launch (start us, length us, event | category | flops | bytes accessed | tf_op | source)
XLA Modules:
  0.0 95.7 jit_solution(766812511539390480)
XLA Ops:
  0.6 92.7 %shard_map.58 = (f32[256,256]{1,0:T(8,128)}, f32[256,256]{1,0:T(8,128)}, f32[8,128]{1,0:T(8,128)}) custom-call(bf16[256,256]{1,0:T(8,128)(2,1)} %sf.1, bf16[256,256]{1,0:T(8,128)(2,1)} %tf_in.1, f32[256,256]{1,0:T(8,128)} %pw.1), custom_call_target="tpu_custom_call" | custom-call | flops 8589934592 | bytes 2097152 | tf_op jit(solution)/shard_map/pallas_call | solution.py:444
  93.3 2.2 %shard_map.59 = (f32[256,256]{1,0:T(8,128)}, f32[256,256]{1,0:T(8,128)}, f32[1,1]{1,0:T(1,128)}) custom-call(bf16[256,256]{1,0:T(8,128)(2,1)} %sf.1, f32[256,256]{1,0:T(8,128)} %pw.1, f32[256,256]{1,0:T(8,128)} %get-tuple-element.9.gs, f32[256,256]{1,0:T(8,128)} %get-tuple-element.10.gp, f32[8,128]{1,0:T(8,128)} %get-tuple-element.11.loss), custom_call_target="tpu_custom_call" | custom-call | tf_op jit(solution)/shard_map/pallas_call | solution.py:473

commit v4 on v3

--- a/solution.py
+++ b/solution.py
@@ -96,6 +96,11 @@
         sent.append(copy)
         return copy
 
+    def drain():
+        for copy in sent:
+            copy.wait_send()
+        sent.clear()
+
     def wait_bytes(ref, sem):
         pltpu.make_async_copy(ref, ref, sem).wait()
 
@@ -170,9 +175,9 @@
             pass_on(U, u_copies)
         teacher_block(lax.rem(z + Z - s + 1, Z))
         teacher_block(lax.rem(z + s - 1, Z))
-    ring_step(H)
     teacher_block(lax.rem(z + Z - H + 1, Z))
     teacher_block(lax.rem(z + H - 1, Z))
+    ring_step(H)
     teacher_block(lax.rem(z + H, Z))
     def col_exchange(k, part_of):
         exchange(col.at[k, part_of], colr.at[k, part_of], z_targets, k + part_of * (2 * SWEEPS + 3))
@@ -199,10 +204,7 @@
         return lax.fori_loop(0, NB, tile, carry, unroll=NB)
 
     lax.fori_loop(0, Z, student_block, 0)
-    used = t_copies[0] + t_copies[1]
-    for copy in used:
-        copy.wait_send()
-    sent[:] = [copy for copy in sent if all(copy is not other for other in used)]
+    drain()
     UT = T
     for b in range(NB):
         UT[b] = U[b].T
@@ -236,7 +238,7 @@
             part[rows] = acc.reshape(R, L)
             return carry
 
-        lax.fori_loop(0, CR // R, tile, 0, unroll=2)
+        lax.fori_loop(0, CR // R, tile, 0, unroll=4)
 
     def col_pass(k, part_of):
         def tile(r, accs):
@@ -247,7 +249,7 @@
                 for i in range(2 * ZH)
             )
 
-        accs = lax.fori_loop(0, CR // R, tile, (jnp.zeros((8, L), F32),) * (2 * ZH), unroll=2)
+        accs = lax.fori_loop(0, CR // R, tile, (jnp.zeros((8, L), F32),) * (2 * ZH), unroll=4)
         for i in range(2 * ZH):
             col[k, part_of, i:i + 1] = jnp.sum(accs[i], axis=0, keepdims=True)
 
@@ -289,6 +291,12 @@
             exchange(stud, studr, xyc_targets, 2 * SWEEPS + 2)
         if k == SWEEPS - 1:
             prepare()
+            for i in range(SWEEPS):
+                for part_of in range(2):
+                    wait_bytes(colr.at[i, part_of], xsem.at[i + part_of * (2 * SWEEPS + 3)])
+            for i in range(SWEEPS - 1):
+                wait_bytes(rowr.at[i], xsem.at[SWEEPS + i])
+            wait_bytes(studr, xsem.at[2 * SWEEPS + 2])
         arrive(slots, SWEEPS + k)
         total = mine[...].astype(F32)
         for i in range(len(xyc_offs)):
@@ -403,8 +411,14 @@
     for i in range(len(xy_offs)):
         total = total + rsr[i].astype(F32)
     gsb[mine] = total
+    early = list(sent)
+    sent.clear()
     y_copies = [send(gsb.at[mine], gsb.at[mine], at_xyc((0, d, 0))) for d in sorted(range(1, Y), key=lambda d: -ring_distance(d, Y))]
 
+    for copy in early:
+        copy.wait_send()
+    wait_bytes(rowr.at[SWEEPS - 1], xsem.at[2 * SWEEPS - 1])
+    wait_bytes(lzr, xsem.at[2 * SWEEPS])
     arrive(lxr, 2 * SWEEPS + 1)
     total = lx[...]
     for i in range(len(xyc_offs)):
@@ -418,14 +432,7 @@
         copy.wait_recv()
     gs_o[...] = gsb[...]
 
-    for copy in sent:
-        copy.wait_send()
-    for k in range(SWEEPS):
-        for part_of in range(2):
-            wait_bytes(colr.at[k, part_of], xsem.at[k + part_of * (2 * SWEEPS + 3)])
-        wait_bytes(rowr.at[k], xsem.at[SWEEPS + k])
-    wait_bytes(studr, xsem.at[2 * SWEEPS + 2])
-    wait_bytes(lzr, xsem.at[2 * SWEEPS])
+    drain()
     wait_bytes(lxr, xsem.at[2 * SWEEPS + 1])
 
 

time: 95.8 us -> 95.3 us (level)
  no operation moved by 1% of the time
where the time goes in v4:
time: 95.3 us; the launch traced here: 95.2 us
  Pallas kernels  94.4 us (99%)
    pallas_call x1, Pallas kernels, shards(): pl.pallas_call(functools.partial(kernel, Z), out_shape=(jax.ShapeDtypeStr...  92.2 us
    pallas_call x1, Pallas kernels, shards(): pl.pallas_call(functools.partial(finish, NB * Z * B), out_shape=(jax.Shap...  2.17 us

profile of v4, /device:TPU:1, one launch (start us, length us, event | category | flops | bytes accessed | tf_op | source)
XLA Modules:
  0.0 95.2 jit_solution(6189353581754355591)
XLA Ops:
  0.6 92.2 %shard_map.58 = (f32[256,256]{1,0:T(8,128)}, f32[256,256]{1,0:T(8,128)}, f32[8,128]{1,0:T(8,128)}) custom-call(bf16[256,256]{1,0:T(8,128)(2,1)} %sf.1, bf16[256,256]{1,0:T(8,128)(2,1)} %tf_in.1, f32[256,256]{1,0:T(8,128)} %pw.1), custom_call_target="tpu_custom_call" | custom-call | flops 8589934592 | bytes 2097152 | tf_op jit(solution)/shard_map/pallas_call | solution.py:451
  92.9 2.2 %shard_map.59 = (f32[256,256]{1,0:T(8,128)}, f32[256,256]{1,0:T(8,128)}, f32[1,1]{1,0:T(1,128)}) custom-call(bf16[256,256]{1,0:T(8,128)(2,1)} %sf.1, f32[256,256]{1,0:T(8,128)} %pw.1, f32[256,256]{1,0:T(8,128)} %get-tuple-element.9.gs, f32[256,256]{1,0:T(8,128)} %get-tuple-element.10.gp, f32[8,128]{1,0:T(8,128)} %get-tuple-element.11.loss), custom_call_target="tpu_custom_call" | custom-call | tf_op jit(solution)/shard_map/pallas_call | solution.py:480

commit v5 on v4

--- a/solution.py
+++ b/solution.py
@@ -298,9 +298,10 @@
                 wait_bytes(rowr.at[i], xsem.at[SWEEPS + i])
             wait_bytes(studr, xsem.at[2 * SWEEPS + 2])
         arrive(slots, SWEEPS + k)
-        total = mine[...].astype(F32)
-        for i in range(len(xyc_offs)):
-            total = total + slots[i].astype(F32)
+        terms = [mine[...].astype(F32)] + [slots[i].astype(F32) for i in range(len(xyc_offs))]
+        while len(terms) > 1:
+            terms = [sum(terms[i + 1:i + 2], terms[i]) for i in range(0, len(terms), 2)]
+        total = terms[0]
         to_rows(cwb, 1.0 / total)
         if k == 1:
             arrive(studr, 2 * SWEEPS + 2)

time: 95.3 us -> 95.3 us (level)
  no operation moved by 1% of the time
where the time goes in v5:
time: 95.3 us; the launch traced here: 95.1 us
  Pallas kernels  94.3 us (99%)
    pallas_call x1, Pallas kernels, shards(): pl.pallas_call(functools.partial(kernel, Z), out_shape=(jax.ShapeDtypeStr...  92.2 us
    pallas_call x1, Pallas kernels, shards(): pl.pallas_call(functools.partial(finish, NB * Z * B), out_shape=(jax.Shap...  2.17 us

profile of v5, /device:TPU:1, one launch (start us, length us, event | category | flops | bytes accessed | tf_op | source)
XLA Modules:
  0.0 95.1 jit_solution(10753981499043341442)
XLA Ops:
  0.6 92.2 %shard_map.58 = (f32[256,256]{1,0:T(8,128)}, f32[256,256]{1,0:T(8,128)}, f32[8,128]{1,0:T(8,128)}) custom-call(bf16[256,256]{1,0:T(8,128)(2,1)} %sf.1, bf16[256,256]{1,0:T(8,128)(2,1)} %tf_in.1, f32[256,256]{1,0:T(8,128)} %pw.1), custom_call_target="tpu_custom_call" | custom-call | flops 8589934592 | bytes 2097152 | tf_op jit(solution)/shard_map/pallas_call | solution.py:452
  92.8 2.2 %shard_map.59 = (f32[256,256]{1,0:T(8,128)}, f32[256,256]{1,0:T(8,128)}, f32[1,1]{1,0:T(1,128)}) custom-call(bf16[256,256]{1,0:T(8,128)(2,1)} %sf.1, f32[256,256]{1,0:T(8,128)} %pw.1, f32[256,256]{1,0:T(8,128)} %get-tuple-element.9.gs, f32[256,256]{1,0:T(8,128)} %get-tuple-element.10.gp, f32[8,128]{1,0:T(8,128)} %get-tuple-element.11.loss), custom_call_target="tpu_custom_call" | custom-call | tf_op jit(solution)/shard_map/pallas_call | solution.py:481
